TPU v7x, 256 devices: a whole 4x4x8 slice. The times are simulated.
256 devices in a mesh: space: 32 (over x, z_hi, core), chan: 8 (over z_lo, y).
Axes of the slice: x: 4, y: 4, z: 8 (z_hi: 4, z_lo: 2; z = z_hi * 2 + z_lo), core: 2. Of those that a mesh axis runs over, the one named last changes fastest.
Arguments:
- features: bfloat16 [64, 16, 16, 1024], P('space', None, None, 'chan'), may hold values from -6 to 6
- slot_tile: int32 [64], replicated, may hold values from 0 to 63, as said below
- land: int32 [64], replicated, may hold values 0 or 1
- dw_kernel: float32 [7, 7, 1024], P(None, None, 'chan'), may hold values from -0.875 to 0.875
- dw_bias: float32 [1024], P('chan'), may hold values from -3 to 3
- ln_gain: float32 [1024], replicated, may hold values from 0.1 to 1.9
- ln_bias: float32 [1024], replicated, may hold values from -3 to 3
- w_in: bfloat16 [1024, 4096], P('space', 'chan'), may hold values from -0.1875 to 0.1875
- b_in: float32 [4096], P('chan'), may hold values from -3 to 3
- w_out: bfloat16 [4096, 1024], P('chan', 'space'), may hold values from -0.09375 to 0.09375
- b_out: float32 [1024], P('chan'), may hold values from -3 to 3
- layer_scale: float32 [1024], P('chan'), may hold values from 0.5 to 1.5
- cotangent: bfloat16 [64, 16, 16, 1024], P('space', None, None, 'chan'), may hold values from -0.1875 to 0.1875
Outputs:
- output: bfloat16 [64, 16, 16, 1024], P('space', None, None, 'chan')
- grad_in_weight: float32 [1024, 4096], P('space', 'chan')
- grad_out_weight: float32 [4096, 1024], P('chan', 'space')
Inputs may be any that keep to these rules, and one draw needn't show every extreme that they name: slot_tile holds each band tile number once.
All inputs are finite; a program needn't handle non-finite values.
Results may differ from a plain program's by a relative error of at most 0.0071.
Values may be sent and summed in bfloat16 or wider, within the bound.
A program may use at most 64 MiB of HBM per device.

v0:
```python
import jax
import jax.numpy as jnp
from jax import lax
from jax.sharding import PartitionSpec as P


def gelu_exact(values):
    return 0.5 * values * (1.0 + jax.scipy.special.erf(values * 0.7071067811865476))


def gelu_slope(values):
    return (
        0.5 * (1.0 + jax.scipy.special.erf(values * 0.7071067811865476))
        + values * jnp.exp(-0.5 * values * values) * 0.3989422804014327
    )


def layer_norm(rows, gain, shift):
    wide = rows.astype(jnp.float32)
    average = jnp.mean(wide, axis=-1, keepdims=True)
    centered = wide - average
    spread = jnp.mean(centered * centered, axis=-1, keepdims=True)
    return (centered * lax.rsqrt(spread + 1e-06) * gain + shift).astype(jnp.bfloat16)


def lookup(table, index):
    positions = jnp.arange(table.shape[0], dtype=jnp.int32)
    return jnp.sum(jnp.where(index[:, None] == positions[None, :], table[None, :], 0), axis=1)


def pad_rows(block):
    return jnp.pad(block, ((0, 0), (3, 3), (0, 0), (0, 0)))


def tap_sum(block, kernel, height, out_width):
    wide = block.astype(jnp.float32)
    summed = jnp.zeros(block.shape[:-3] + (height, out_width, block.shape[-1]), jnp.float32)
    for row in range(7):
        for col in range(7):
            summed = (
                summed + kernel[row, col] * wide[..., row : row + height, col : col + out_width, :]
            )
    return summed


def convolve(block, kernel, height, out_width):
    return tap_sum(block, kernel, height, out_width)


def body(
    features,
    slot_tile,
    land,
    dw_kernel,
    dw_bias,
    ln_gain,
    ln_bias,
    w_in,
    b_in,
    w_out,
    b_out,
    layer_scale,
    cotangent,
):
    tile_count, height, width, chans = features.shape
    total_tiles = slot_tile.shape[0]
    first_slot = lax.axis_index("space") * tile_count
    my_tiles = lax.dynamic_slice_in_dim(slot_tile, first_slot, tile_count)
    land_tiles = lookup(land, my_tiles)
    land_scale = land_tiles.astype(jnp.float32)[:, None, None, None]
    masked = features * land_scale.astype(jnp.bfloat16)
    strips = jnp.stack((masked[:, :, :3, :], masked[:, :, width - 3 :, :]), axis=1)
    everyone = lax.all_gather(strips, "space", axis=0, tiled=True)
    slot_ids = jnp.arange(total_tiles, dtype=jnp.int32)
    inverse = jnp.sum(
        jnp.where(slot_tile[None, :] == slot_ids[:, None], slot_ids[None, :], 0), axis=1
    )
    left_slot = lookup(inverse, my_tiles - 1)
    right_slot = lookup(inverse, my_tiles + 1)
    has_left = (my_tiles > 0).astype(jnp.bfloat16)[:, None, None, None]
    has_right = (my_tiles < total_tiles - 1).astype(jnp.bfloat16)[:, None, None, None]
    from_left = everyone[left_slot, 1] * has_left
    from_right = everyone[right_slot, 0] * has_right
    conv = convolve(
        pad_rows(jnp.concatenate((from_left, masked, from_right), axis=2)), dw_kernel, height, width
    )
    dconv = (conv + dw_bias).astype(jnp.bfloat16)
    gathered = lax.all_gather(dconv, "chan", axis=3, tiled=True)
    normed = layer_norm(gathered.reshape(-1, gathered.shape[-1]), ln_gain, ln_bias)
    pre = (
        jnp.dot(
            normed,
            lax.all_gather(w_in, "space", axis=0, tiled=True),
            preferred_element_type=jnp.float32,
        )
        + b_in
    )
    hidden = gelu_exact(pre).astype(jnp.bfloat16)
    w_out_full = lax.all_gather(w_out, "space", axis=1, tiled=True)
    partial_value = jnp.dot(hidden, w_out_full, preferred_element_type=jnp.float32)
    mixed = lax.psum_scatter(partial_value, "chan", scatter_dimension=1, tiled=True)
    row_land = jnp.broadcast_to(land_scale, (tile_count, height, width, 1)).reshape(-1, 1)
    result = row_land * (
        features.reshape(-1, chans).astype(jnp.float32) + layer_scale * (mixed + b_out)
    )
    output = result.astype(jnp.bfloat16).reshape(features.shape)
    slope = (cotangent.reshape(-1, chans).astype(jnp.float32) * row_land * layer_scale).astype(
        jnp.bfloat16
    )
    slope_full = lax.all_gather(slope, "chan", axis=1, tiled=True)
    contract_rows = (((0,), (0,)), ((), ()))
    grad_out_local = lax.dot_general(
        hidden, slope_full, contract_rows, preferred_element_type=jnp.float32
    )
    back = (
        lax.dot_general(
            slope_full, w_out_full, (((1,), (1,)), ((), ())), preferred_element_type=jnp.float32
        )
        * gelu_slope(pre)
    ).astype(jnp.bfloat16)
    grad_in_local = lax.dot_general(normed, back, contract_rows, preferred_element_type=jnp.float32)
    grad_in, grad_out = (
        lax.psum_scatter(grad_in_local, "space", scatter_dimension=0, tiled=True),
        lax.psum_scatter(grad_out_local, "space", scatter_dimension=1, tiled=True),
    )
    return (output, grad_in, grad_out)


def solution(mesh):
    return jax.shard_map(
        body,
        mesh=mesh,
        in_specs=(
            P("space", None, None, "chan"),
            P(),
            P(),
            P(None, None, "chan"),
            P("chan"),
            P(),
            P(),
            P("space", "chan"),
            P("chan"),
            P("chan", "space"),
            P("chan"),
            P("chan"),
            P("space", None, None, "chan"),
        ),
        out_specs=(P("space", None, None, "chan"), P("space", "chan"), P("chan", "space")),
        check_vma=False,
    )
```

profile of v0, /device:TPU:1, one launch (start us, length us, event | category | flops | bytes accessed | tf_op | source)
XLA Modules:
  0.0 502.9 jit_solution(17019567223189783239)
XLA Ops:
  7.2 0.7 compare_convert_fusion.1
  7.9 0.8 fusion.76
  8.8 1.0 broadcast_multiply_fusion
  9.9 0.6 copy.30
  10.5 0.0 all-gather.8.cloned.1.call-start
  10.6 0.8 select_reduce_fusion
  11.4 0.2 fusion.77
  11.6 0.9 slice_bitcast_fusion.48
  12.5 1.0 slice_bitcast_fusion.50
  13.5 1.0 slice_bitcast_fusion.49
  14.5 54.0 %all-gather.6.cloned.1.call-done = bf16[64,2,16,3,128]{4,2,3,1,0:T(8,128)(2,1)} async-done(((bf16[2,2,16,3,128]{4,2,3,1,0:T(8,128)(2,1)}), bf16[64,2,16,3,128]{4,2,3,1,0:T(8,128)(2,1)}) %all-gather.6.cloned.1.call-update) | async-done | bytes 1572880 | tf_op jit(solution)/shard_map/all_gather | solution.py:73
  68.5 2.0 gather_fusion.1
  70.5 0.1 broadcast_multiply_fusion.1
  70.6 2.0 gather_fusion
  72.5 0.1 broadcast_multiply_fusion.2
  72.6 0.1 fusion.21
  72.7 3.1 fusion.24
  75.9 0.0 all-gather.10.cloned.1.call-start
  75.9 0.7 all-gather.10.cloned.1.call-update
  76.7 0.5 all-gather.12.cloned.1.call-update
  77.2 0.0 reduce-scatter.4.cloned.1.call-start
  77.3 31.6 %all-gather.8.cloned.1.call-done = bf16[2,16,16,1024]{3,2,1,0:T(8,128)(2,1)} async-done(((bf16[2,16,16,128]{3,2,1,0:T(8,128)(2,1)}), bf16[2,16,16,1024]{3,2,1,0:T(8,128)(2,1)}) %all-gather.8.cloned.1.call-update) | async-done | bytes 1048592 | tf_op jit(solution)/shard_map/all_gather | solution.py:88
  108.9 1.5 convert_reduce_fusion
  110.4 0.1 copy.38
  110.5 0.1 copy.34
  110.5 0.1 div.9
  110.6 1.6 multiply_reduce_fusion
  112.3 0.1 copy.39
  112.4 0.1 copy.37
  112.4 0.1 rsqrt.12
  112.5 0.4 fusion.3
  113.0 55.8 %all-gather.10.cloned.1.call-done = bf16[1024,512]{1,0:T(8,128)(2,1)} async-done(((bf16[32,512]{1,0:T(8,128)(2,1)}), bf16[1024,512]{1,0:T(8,128)(2,1)}) %all-gather.10.cloned.1.call-update) | async-done | bytes 1048592 | tf_op jit(solution)/shard_map/all_gather | solution.py:93
  168.8 3.0 multiply_convert_fusion
  171.8 48.9 %all-gather.12.cloned.1.call-done = bf16[512,1024]{0,1:T(8,128)(2,1)} async-done(((bf16[512,32]{0,1:T(8,128)(2,1)}), bf16[512,1024]{0,1:T(8,128)(2,1)}) %all-gather.12.cloned.1.call-update) | async-done | bytes 1048592 | tf_op jit(solution)/shard_map/all_gather | solution.py:99
  220.7 3.3 fusion.90
  224.1 0.0 all-gather.14.cloned.1.call-start
  224.1 0.1 broadcast_in_dim.40
  224.2 0.1 broadcast_in_dim.41
  224.3 36.9 %reduce-scatter.4.cloned.1.call-done = f32[512,128]{1,0:T(8,128)} async-done(((f32[512,1024]{1,0:T(8,128)}), f32[512,128]{1,0:T(8,128)}) %reduce-scatter.4.cloned.1.call-update) | async-done | bytes 262160 | tf_op jit(solution)/shard_map/reduce_scatter | solution.py:101
  261.2 1.8 fusion.73
  263.0 0.0 reduce-scatter.6.cloned.1.call-start
  263.1 40.5 %all-gather.14.cloned.1.call-done = bf16[512,1024]{1,0:T(8,128)(2,1)} async-done(((bf16[512,128]{1,0:T(8,128)(2,1)}), bf16[512,1024]{1,0:T(8,128)(2,1)}) %all-gather.14.cloned.1.call-update) | async-done | bytes 1048592 | tf_op jit(solution)/shard_map/all_gather | solution.py:110
  303.6 4.5 fusion.5
  308.1 0.0 reduce-scatter.8.cloned.1.call-start
  308.1 1.1 copy-done.2
  309.3 2.1 fusion.91
  311.4 91.1 %reduce-scatter.6.cloned.1.call-done = f32[32,512]{1,0:T(8,128)} async-done(((f32[1024,512]{1,0:T(8,128)}), f32[32,512]{1,0:T(8,128)}) %reduce-scatter.6.cloned.1.call-update) | async-done | bytes 65552 | tf_op jit(solution)/shard_map/reduce_scatter | solution.py:123
  402.5 93.6 %reduce-scatter.8.cloned.1.call-done = f32[512,32]{0,1:T(8,128)} async-done(((f32[512,1024]{0,1:T(8,128)}), f32[512,32]{0,1:T(8,128)}) %reduce-scatter.8.cloned.1.call-update) | async-done | bytes 65552 | tf_op jit(solution)/shard_map/reduce_scatter | solution.py:124
  (37 shorter events, 0.4 us)
Async XLA Ops:
  7.2 61.3 %all-gather.6.cloned.1.call-start = ((), (), s32[]{:S(2)}) async-start(), calls=%async_computation.3 | async-start | bytes 1622016 | tf_op jit(solution)/shard_map/all_gather | solution.py:73
  10.5 98.3 %all-gather.8.cloned.1.call-start = ((), (), s32[]{:S(2)}) async-start(), calls=%async_computation.4 | async-start | bytes 1179648 | tf_op jit(solution)/shard_map/all_gather | solution.py:88
  75.9 36.6 %copy-start.5 = (f32[1024]{0:T(1024)S(1)}, f32[1024]{0:T(1024)}, u32[]{:S(2)}) copy-start(f32[1024]{0:T(1024)} %param.19) | copy-start | bytes 12292
  75.9 36.7 %copy-start.6 = (f32[1024]{0:T(1024)S(1)}, f32[1024]{0:T(1024)}, u32[]{:S(2)}) copy-start(f32[1024]{0:T(1024)} %param.18) | copy-start | bytes 12292
  75.9 92.9 %all-gather.10.cloned.1.call-start = ((), (), s32[]{:S(2)}) async-start(), calls=%async_computation.5 | async-start | bytes 1081344 | tf_op jit(solution)/shard_map/all_gather | solution.py:93
  76.6 144.1 %all-gather.12.cloned.1.call-start = ((), (), s32[]{:S(2)}) async-start(), calls=%async_computation.6 | async-start | bytes 1081344 | tf_op jit(solution)/shard_map/all_gather | solution.py:99
  77.2 91.6 %copy-start.9 = (f32[512]{0:T(512)S(1)}, f32[512]{0:T(512)}, u32[]{:S(2)}) copy-start(f32[512]{0:T(512)} %param.21) | copy-start | bytes 6148
  77.2 184.0 %reduce-scatter.4.cloned.1.call-start = ((), (), s32[]{:S(2)}) async-start(), calls=%async_computation.7 | async-start | bytes 2359296 | tf_op jit(solution)/shard_map/reduce_scatter | solution.py:101
  108.8 3.7 copy-start
  220.7 40.5 %copy-start.3 = (bf16[2,16,16,128]{3,2,1,0:T(8,128)(2,1)S(1)}, bf16[2,16,16,128]{3,2,1,0:T(8,128)(2,1)}, u32[]{:S(2)}) copy-start(bf16[2,16,16,128]{3,2,1,0:T(8,128)(2,1)} %param.13) | copy-start | bytes 393220
  220.7 40.5 %copy-start.4 = (bf16[2,16,16,128]{3,2,1,0:T(8,128)(2,1)S(1)}, bf16[2,16,16,128]{3,2,1,0:T(8,128)(2,1)}, u32[]{:S(2)}) copy-start(bf16[2,16,16,128]{3,2,1,0:T(8,128)(2,1)} %param.25) | copy-start | bytes 393220
  220.7 40.5 %copy-start.7 = (f32[128]{0:T(128)S(1)}, f32[128]{0:T(128)}, u32[]{:S(2)}) copy-start(f32[128]{0:T(128)} %param.24) | copy-start | bytes 1540
  220.7 40.5 %copy-start.8 = (f32[128]{0:T(128)S(1)}, f32[128]{0:T(128)}, u32[]{:S(2)}) copy-start(f32[128]{0:T(128)} %param.23) | copy-start | bytes 1540
  224.1 79.5 %copy-start.1 = (bf16[512,1024]{0,1:T(8,128)(2,1)S(1)}, bf16[512,1024]{0,1:T(8,128)(2,1)}, u32[]{:S(2)}) copy-start(bf16[512,1024]{0,1:T(8,128)(2,1)} %all-gather.12.cloned.1.call-done) | copy-start | bytes 3145732
  224.1 79.5 %all-gather.14.cloned.1.call-start = ((), (), s32[]{:S(2)}) async-start(), calls=%async_computation.8 | async-start | bytes 1179648 | tf_op jit(solution)/shard_map/all_gather | solution.py:110
  263.0 139.5 %reduce-scatter.6.cloned.1.call-start = ((), (), s32[]{:S(2)}) async-start(), calls=%async_computation.9 | async-start | bytes 2162688 | tf_op jit(solution)/shard_map/reduce_scatter | solution.py:123
  308.0 1.2 copy-start.2
  308.1 188.0 %reduce-scatter.8.cloned.1.call-start = ((), (), s32[]{:S(2)}) async-start(), calls=%async_computation.10 | async-start | bytes 2162688 | tf_op jit(solution)/shard_map/reduce_scatter | solution.py:124
Sparse Core Ops, SparseCore 0:
  11.1 57.3 all-gather.5
  76.0 32.7 all-gather.7
  111.4 57.3 all-gather.9
  171.2 49.4 all-gather.11
  224.2 36.9 reduce-scatter.3
  263.1 40.3 all-gather.13
  308.2 94.2 reduce-scatter.5
  406.9 89.1 reduce-scatter.7
where the time goes:
time: 505 us; the launch traced here: 503 us
  waiting for transfers between devices  454 us (90%)
  between operations  14.3 us (3%)
  matrix products  12.9 us (3%)
  other arithmetic  12.4 us (2%)
  local copies, waits for them, and re-layouts  9.29 us (2%)
    reduce_scatter x1, waiting for transfers between devices, body(): lax.psum_scatter(grad_out_local, 'space', scatter_dimension=1, tiled=True)  93.6 us
    reduce_scatter x1, waiting for transfers between devices, body(): lax.psum_scatter(grad_in_local, 'space', scatter_dimension=0, tiled=True)  91.1 us
    all_gather x1, waiting for transfers between devices, body(): lax.all_gather(w_in, 'space', axis=0, tiled=True)  55.8 us
    all_gather x1, waiting for transfers between devices, body(): everyone = lax.all_gather(strips, 'space', axis=0, tiled=True)  54 us
    all_gather x1, waiting for transfers between devices, body(): w_out_full = lax.all_gather(w_out, 'space', axis=1, tiled=True)  48.9 us
    all_gather x1, waiting for transfers between devices, body(): slope_full = lax.all_gather(slope, 'chan', axis=1, tiled=True)  40.5 us
    reduce_scatter x1, waiting for transfers between devices, body(): lax.psum_scatter(partial_value, 'chan', scatter_dimension=1, tiled=True)  36.9 us
    all_gather x1, waiting for transfers between devices, body(): gathered = lax.all_gather(dconv, 'chan', axis=3, tiled=True)  31.6 us
  transfers between devices with their start and end apart: 8, of which 8 were waited for; matrix products, arithmetic and copies ran while one was open for 3% of the time, Pallas kernels for 0%

commit v1 on v0

v1 whole, which is shorter than its diff:
```python
import jax
import jax.numpy as jnp
from jax import lax
from jax.experimental import pallas as pl
from jax.experimental.pallas import tpu as pltpu
from jax.sharding import PartitionSpec as P

MESH = pl.DeviceIdType.MESH
F32, BF16 = jnp.float32, jnp.bfloat16
FAR = (1, 3, 2)
COPIES = 110


def wrap4(value):
    return lax.rem(value + 4, 4)


class Place:
    def __init__(self):
        self.space, self.chan = lax.axis_index("space"), lax.axis_index("chan")
        self.x, self.zh, self.core = self.space // 8, (self.space // 2) % 4, self.space % 2
        self.zl, self.y = self.chan // 4, self.chan % 4

    def slot(self, dx=0, dz=0, other=False):
        core = 1 - self.core if other else self.core
        return wrap4(self.x + dx) * 8 + wrap4(self.zh + dz) * 2 + core

    def part(self, dy=0, other=False):
        return (1 - self.zl if other else self.zl) * 4 + wrap4(self.y + dy)

    def peers(self):
        ids = [(self.slot(dz=d), self.chan) for d in (1, 2, 3)]
        ids += [(self.slot(dx=d), self.chan) for d in (1, 2, 3)]
        ids += [(self.slot(other=True), self.chan), (self.space, self.part(other=True))]
        return ids + [(self.space, self.part(dy=d)) for d in (1, 2, 3)]


class Links:
    def __init__(self, send_sems, recv_sems):
        self.send_sems, self.recv_sems, self.sent = send_sems, recv_sems, []

    def describe(self, number, source, target, device):
        return pltpu.make_async_remote_copy(
            src_ref=source,
            dst_ref=target,
            send_sem=self.send_sems.at[number],
            recv_sem=self.recv_sems.at[number],
            device_id=device,
            device_id_type=MESH,
        )

    def start(self, source, target, device):
        number = len(self.sent)
        assert number < COPIES
        copy = self.describe(number, source, target, device)
        copy.start()
        self.sent.append(copy)
        return number, device

    def landed(self, ticket, where):
        self.describe(ticket[0], where, where, ticket[1]).wait_recv()

    def finish(self):
        for copy in self.sent:
            copy.wait_send()


class SpaceGather:
    def __init__(self, links, place, block, use=lambda s: None):
        self.links, self.place, self.block, self.use = links, place, block, use
        self.over_z, self.over_x, self.over_core = {}, {}, {}

    def send(self, block, device):
        return self.links.start(block, block, device)

    def own_z(self):
        place = self.place
        mine = self.block(place.slot())
        for d in FAR:
            self.over_z[d] = self.send(mine, (place.slot(dz=d), place.chan))

    def spread(self, d):
        place = self.place
        block = self.block(place.slot(dz=-d))
        if d:
            self.links.landed(self.over_z[d], block)
        for e in FAR:
            self.over_x[d, e] = self.send(block, (place.slot(dx=e), place.chan))
        self.over_core[d, 0] = self.send(block, (place.slot(other=True), place.chan))
        self.use(place.slot(dz=-d))

    def cross(self, d, e):
        place = self.place
        block = self.block(place.slot(dx=-e, dz=-d))
        self.links.landed(self.over_x[d, e], block)
        self.over_core[d, e] = self.send(block, (place.slot(other=True), place.chan))
        self.use(place.slot(dx=-e, dz=-d))

    def wait(self):
        place = self.place
        for (d, e), ticket in self.over_core.items():
            self.links.landed(ticket, self.block(place.slot(dx=-e, dz=-d, other=True)))
            self.use(place.slot(dx=-e, dz=-d, other=True))


class ChanGather:
    def __init__(self, links, place, block):
        self.links, self.place, self.block = links, place, block
        self.over_y = {}

    def own(self):
        place = self.place
        mine = self.block(place.part())
        self.over_zl = self.links.start(mine, mine, (place.space, place.part(other=True)))
        self.spread(mine, False)

    def spread(self, block, other):
        place = self.place
        for d in FAR:
            self.over_y[d, other] = self.links.start(block, block, (place.space, place.part(dy=d)))

    def cross(self):
        block = self.block(self.place.part(other=True))
        self.links.landed(self.over_zl, block)
        self.spread(block, True)

    def wait(self):
        for (d, other), ticket in self.over_y.items():
            self.links.landed(ticket, self.block(self.place.part(dy=-d, other=other)))


def kernel(
    slot_tile, land, feat, cot, dw, dw_bias, gain, shift, w_in, b_in, w_out, b_out, scale,
    out, gin, gout,
    xpad, hbuf, hacc, wbuf, sbuf, cbuf, dbuf0, dbuf1, nbuf, pre, qbuf, hid, back,
    gacc, gsend, gcore, gxs, gxr, gown, gzs, gzr, msend, mrecv, mown, mzs, mzr,
    send_sems, recv_sems,
):
    place, links = Place(), Links(send_sems, recv_sems)
    core, zl = place.core, place.zl
    first = place.space * 2

    xpad[...] = jnp.zeros_like(xpad)
    tiles = [slot_tile[first + t] for t in range(2)]
    lands = [land[tile].astype(F32) for tile in tiles]
    for t in range(2):
        masked = feat[t * 256 : (t + 1) * 256, :].astype(F32) * lands[t]
        xpad[t, 3:19, 8:24, :] = masked.reshape(16, 16, 128)
        for side, begin in ((0, 0), (1, 13)):
            for q in range(3):
                column = xpad[t, 3:19, 8 + begin + q, :]
                hbuf[first * 2 + t * 2 + side, q] = column.astype(BF16)
    for t in range(2):
        rows = slice(t * 256, (t + 1) * 256)
        sbuf[place.chan, rows] = (cot[rows, :].astype(F32) * lands[t] * scale[...]).astype(BF16)
    wbuf[place.space, 0] = w_in[...]
    wide = jnp.concatenate((w_out[...].astype(F32), jnp.zeros((512, 96), F32)), axis=1)
    wbuf[place.space, 1] = wide.T[:32].astype(BF16)
    barrier = pltpu.get_barrier_semaphore()
    for peer in place.peers():
        pl.semaphore_signal(barrier, inc=1, device_id=peer, device_id_type=MESH)
    pl.semaphore_wait(barrier, len(place.peers()))

    hacc[...] = jnp.zeros((2, 2, 3, 16, 128), F32)

    def pick(s):
        held = [slot_tile[s * 2 + i] for i in range(2)]
        for t in range(2):
            for side, step in ((0, -1), (1, 1)):
                for i in range(2):
                    chosen = (held[i] == tiles[t] + step).astype(F32)
                    hacc[t, side] += hbuf[s * 4 + i * 2 + 1 - side].astype(F32) * chosen

    halos = SpaceGather(links, place, lambda s: hbuf.at[pl.ds(s * 4, 4)], pick)
    weights = SpaceGather(links, place, lambda s: wbuf.at[s])
    slopes = ChanGather(links, place, lambda c: sbuf.at[c])
    dbufs = (dbuf0, dbuf1)
    convs = [ChanGather(links, place, lambda c, held=held: held.at[c]) for held in dbufs]

    halos.own_z()
    halos.spread(0)
    slopes.own()

    for d in FAR:
        halos.spread(d)
    slopes.cross()
    weights.own_z()
    for d in (0,) + FAR:
        for e in FAR:
            halos.cross(d, e)
    weights.spread(0)
    halos.wait()

    for t in range(2):
        for q in range(3):
            xpad[t, 3:19, 5 + q, :] = hacc[t, 0, q]
            xpad[t, 3:19, 24 + q, :] = hacc[t, 1, q]
    for t in range(2):

        def half(h, carry):
            total = jnp.zeros((8, 16, 128), F32)
            for e in range(7):
                rows = xpad[t, pl.ds(h * 8, 14), 5 + e : 21 + e, :]
                for a in range(7):
                    total = total + dw[a, e : e + 1, :][None] * rows[a : a + 8]
            total = total + dw_bias[...][None]
            cbuf[t, pl.ds(pl.multiple_of(h * 128, 128), 128)] = total.reshape(128, 128).astype(BF16)
            return carry

        lax.fori_loop(0, 2, half, 0)
        dbufs[t][place.chan] = cbuf[t]
        convs[t].own()

    for d in FAR:
        weights.spread(d)
    convs[0].cross()
    convs[1].cross()
    for d in (0,) + FAR:
        for e in FAR:
            weights.cross(d, e)
    slopes.wait()
    weights.wait()

    for t in range(2):
        rows = slice(t * 256, (t + 1) * 256)
        slope_rows = jnp.concatenate([sbuf[c, rows] for c in range(8)], axis=1)
        qbuf[rows] = jnp.dot(
            slope_rows, wbuf[:, 1].reshape(1024, 512), preferred_element_type=F32
        )

    for t in range(2):
        convs[t].wait()

        def norm(i, carry):
            at = pl.ds(pl.multiple_of(i * 64, 64), 64)
            x = dbufs[t][:, at, :].astype(F32)
            mean = jnp.sum(jnp.sum(x, axis=0), axis=1, keepdims=True) * (1.0 / 1024)
            x = x - mean[None]
            spread = jnp.sum(jnp.sum(x * x, axis=0), axis=1, keepdims=True) * (1.0 / 1024)
            x = x * lax.rsqrt(spread + 1e-06)[None]
            to = pl.ds(pl.multiple_of(t * 256 + i * 64, 64), 64)
            for c in range(8):
                y = x[c] * gain[c : c + 1] + shift[c : c + 1]
                nbuf[to, c * 128 : (c + 1) * 128] = y.astype(BF16)
            return carry

        lax.fori_loop(0, 4, norm, 0)
        rows = slice(t * 256, (t + 1) * 256)
        pre[...] = (
            jnp.dot(nbuf[rows], wbuf[:, 0].reshape(1024, 512), preferred_element_type=F32)
            + b_in[...]
        )

        def act(i, carry):
            at = pl.ds(pl.multiple_of(i * 32, 32), 32)
            to = pl.ds(pl.multiple_of(t * 256 + i * 32, 32), 32)
            p = pre[at]
            below = 0.5 * (1.0 + lax.erf(p * 0.7071067811865476))
            hid[to] = (p * below).astype(BF16)
            rise = below + p * jnp.exp(-0.5 * p * p) * 0.3989422804014327
            back[to] = (qbuf[to] * rise).astype(BF16)
            return carry

        lax.fori_loop(0, 8, act, 0)

    over_core = {}
    for g in (1, 0):
        for i in range(4):
            if g:
                left = jnp.concatenate((sbuf[2 * i], sbuf[2 * i + 1]), axis=1)
            else:
                left = nbuf[:, i * 256 : (i + 1) * 256]
            summed = lax.dot_general(
                left, (hid if g else back)[...], (((0,), (0,)), ((), ())),
                preferred_element_type=F32,
            )
            gacc[g, 4 * i : 4 * i + 4] = summed.reshape(4, 2, 32, 512)
            gsend[g, 4 * i : 4 * i + 4] = gacc[g, 4 * i : 4 * i + 4, 1 - core].astype(BF16)
        over_core[g] = links.start(
            gsend.at[g], gcore.at[g], (place.slot(other=True), place.chan)
        )

    mixed_y = {}
    for d in FAR + (0,):
        to = wrap4(place.y + d)
        columns = jnp.concatenate(
            [wbuf[pl.ds(k * 16 + to * 4, 4), 1].reshape(128, 512) for k in range(2)], axis=0
        )
        partial = lax.dot_general(
            hid[...], columns, (((1,), (1,)), ((), ())), preferred_element_type=F32
        )
        for k in range(2):
            piece = partial[:, k * 128 : (k + 1) * 128]
            if d:
                msend[d - 1, k] = piece.astype(BF16)
            else:
                mown[k] = piece
        if d:
            mixed_y[d] = links.start(
                msend.at[d - 1], mrecv.at[d - 1], (place.space, place.part(dy=d))
            )

    over_x, over_z = {}, {}
    for g in (1, 0):
        links.landed(over_core[g], gcore.at[g])
        for d in FAR:
            at = pl.ds(wrap4(place.x + d) * 4, 4)
            gxs[g, d - 1] = (gacc[g, at, core] + gcore[g, at].astype(F32)).astype(BF16)
            over_x[g, d] = links.start(
                gxs.at[g, d - 1], gxr.at[g, d - 1], (place.slot(dx=d), place.chan)
            )
    for d in FAR:
        links.landed(mixed_y[d], mrecv.at[d - 1])
    for d in FAR:
        mown[...] += mrecv[d - 1].astype(F32)
    mzs[...] = mown[1 - zl].astype(BF16)
    mixed_z = links.start(mzs, mzr, (place.space, place.part(other=True)))
    for g in (1, 0):
        at = pl.ds(place.x * 4, 4)
        gown[g] = gacc[g, at, core] + gcore[g, at].astype(F32)
        for d in FAR:
            links.landed(over_x[g, d], gxr.at[g, d - 1])
            gown[g] += gxr[g, d - 1].astype(F32)
        for d in FAR:
            gzs[g, d - 1] = gown[g, wrap4(place.zh + d)].astype(BF16)
            over_z[g, d] = links.start(
                gzs.at[g, d - 1], gzr.at[g, d - 1], (place.slot(dz=d), place.chan)
            )
    links.landed(mixed_z, mzr)
    for t in range(2):
        rows = slice(t * 256, (t + 1) * 256)
        mixed = mown[zl, rows] + mzr[rows].astype(F32)
        value = feat[rows, :].astype(F32) + scale[...] * (mixed + b_out[...])
        out[rows, :] = (lands[t] * value).astype(BF16)
    for g, result in ((1, gout), (0, gin)):
        total = gown[g, place.zh]
        for d in FAR:
            links.landed(over_z[g, d], gzr.at[g, d - 1])
            total = total + gzr[g, d - 1].astype(F32)
        result[...] = total
    links.finish()


def body(
    features, slot_tile, land, dw_kernel, dw_bias, ln_gain, ln_bias, w_in, b_in, w_out, b_out,
    layer_scale, cotangent,
):
    vmem = pl.BlockSpec(memory_space=pltpu.VMEM)
    smem = pl.BlockSpec(memory_space=pltpu.SMEM)
    scratch = [
        ((2, 22, 32, 128), F32),
        ((128, 3, 16, 128), BF16),
        ((2, 2, 3, 16, 128), F32),
        ((32, 2, 32, 512), BF16),
        ((8, 512, 128), BF16),
        ((2, 256, 128), BF16),
        ((8, 256, 128), BF16),
        ((8, 256, 128), BF16),
        ((512, 1024), BF16),
        ((256, 512), F32),
        ((512, 512), F32),
        ((512, 512), BF16),
        ((512, 512), BF16),
        ((2, 16, 2, 32, 512), F32),
        ((2, 16, 32, 512), BF16),
        ((2, 16, 32, 512), BF16),
        ((2, 3, 4, 32, 512), BF16),
        ((2, 3, 4, 32, 512), BF16),
        ((2, 4, 32, 512), F32),
        ((2, 3, 32, 512), BF16),
        ((2, 3, 32, 512), BF16),
        ((3, 2, 512, 128), BF16),
        ((3, 2, 512, 128), BF16),
        ((2, 512, 128), F32),
        ((512, 128), BF16),
        ((512, 128), BF16),
    ]
    output, grad_in, grad_out = pl.pallas_call(
        kernel,
        out_shape=(
            jax.ShapeDtypeStruct((512, 128), BF16),
            jax.ShapeDtypeStruct((32, 512), F32),
            jax.ShapeDtypeStruct((32, 512), F32),
        ),
        in_specs=[smem, smem] + [vmem] * 11,
        out_specs=(vmem, vmem, vmem),
        scratch_shapes=[pltpu.VMEM(shape, dtype) for shape, dtype in scratch]
        + [pltpu.SemaphoreType.DMA((COPIES,)), pltpu.SemaphoreType.DMA((COPIES,))],
        compiler_params=pltpu.CompilerParams(
            collective_id=0, has_side_effects=True, vmem_limit_bytes=48 * 2**20
        ),
        name="block",
    )(
        slot_tile,
        land,
        features.reshape(512, 128),
        cotangent.reshape(512, 128),
        dw_kernel,
        dw_bias.reshape(1, 128),
        ln_gain.reshape(8, 128),
        ln_bias.reshape(8, 128),
        w_in,
        b_in.reshape(1, 512),
        w_out,
        b_out.reshape(1, 128),
        layer_scale.reshape(1, 128),
    )
    return output.reshape(features.shape), grad_in, grad_out.T


def solution(mesh):
    return jax.shard_map(
        body,
        mesh=mesh,
        in_specs=(
            P("space", None, None, "chan"),
            P(),
            P(),
            P(None, None, "chan"),
            P("chan"),
            P(),
            P(),
            P("space", "chan"),
            P("chan"),
            P("chan", "space"),
            P("chan"),
            P("chan"),
            P("space", None, None, "chan"),
        ),
        out_specs=(P("space", None, None, "chan"), P("space", "chan"), P("chan", "space")),
        check_vma=False,
    )
```

time: 505 us -> 77 us (0.15)
  waiting for transfers between devices: 454 us -> 0 us
  Pallas kernels: 0 us -> 70.5 us
  between operations: 14.3 us -> 0.81 us
  matrix products: 12.9 us -> 0 us
  other arithmetic: 12.4 us -> 0 us
    all_gather x5 -> x0, waiting for transfers between devices: 231 us -> none  [the longest x1 55.8 us: body(): lax.all_gather(w_in, 'space', axis=0, tiled=True)]
    reduce_scatter x3 -> x0, waiting for transfers between devices: 222 us -> none  [the longest x1 93.6 us: body(): lax.psum_scatter(grad_out_local, 'space', scatter_dimension=1, tiled=True)]
    pallas_call x0 -> x1, Pallas kernels: none -> 70.5 us  [body(): pl.pallas_call(kernel, out_shape=(jax.ShapeDtypeStruct((512, 128), BF16),...]
    dot_general x4 -> x0, matrix products: 12.9 us -> none  [the longest x1 4.45 us: body(): lax.dot_general(normed, back, contract_rows, preferred_element_type=jnp.f...]
    convert_element_type x7 -> x0, other arithmetic: 6.23 us -> none  [the longest x1 3.13 us: body(): dconv = (conv + dw_bias).astype(jnp.bfloat16)]
  transfers between devices with their start and end apart: 8 -> 0, of which waited for: 8 -> 0; matrix products, arithmetic and copies ran while one was open for 3% -> 0% of each run, Pallas kernels for 0% -> 0%
where the time goes in v1:
time: 77 us; the launch traced here: 75.9 us
  Pallas kernels  70.5 us (92%)
  local copies, waits for them, and re-layouts  4.59 us (6%)
  between operations  0.81 us (1%)
    pallas_call x1, Pallas kernels, body(): pl.pallas_call(kernel, out_shape=(jax.ShapeDtypeStruct((512, 128), BF16),...  70.5 us
    unnamed x28, local copies, waits for them, and re-layouts  4.59 us

profile of v1, /device:TPU:1, one launch (start us, length us, event | category | flops | bytes accessed | tf_op | source)
XLA Modules:
  0.0 75.9 jit_solution(16134340385192653223)
XLA Ops:
  0.6 0.0 copy-start
  0.6 0.0 copy-start.2
  0.7 0.0 copy-start.4
  0.7 0.0 copy-start.5
  0.7 0.0 copy-start.6
  0.7 0.0 copy-start.7
  0.7 0.0 copy-start.8
  0.7 0.0 copy-start.9
  0.7 0.0 copy-start.10
  0.7 0.0 copy-start.11
  0.7 1.0 %copy.16.w_out = bf16[512,32]{1,0:T(8,128)(2,1)S(1)} copy(bf16[512,32]{0,1:T(8,128)(2,1)} %param.22) | data formatting | bytes 65536 | tf_op args[9]
  1.7 0.0 copy-done
  1.7 0.0 copy-done.2
  1.7 0.0 copy-done.4
  1.7 0.0 copy-done.5
  1.8 0.0 copy-done.6
  1.8 0.0 copy-done.7
  1.8 0.0 copy-done.8
  1.8 0.0 copy-done.9
  1.8 0.0 copy-done.10
  1.8 0.0 copy-done.11
  1.8 0.0 copy-start.1
  1.8 0.9 %copy-done.1 = bf16[2,16,16,128]{3,2,1,0:T(8,128)(2,1)S(1)} copy-done((bf16[2,16,16,128]{3,2,1,0:T(8,128)(2,1)S(1)}, bf16[2,16,16,128]{3,2,1,0:T(8,128)(2,1)}, u32[]{:S(2)}) %copy-start.1) | copy-done | bytes 131096
  2.7 0.0 copy-start.3
  2.7 0.7 copy-done.3
  3.5 70.5 %block.1 = (bf16[512,128]{1,0:T(8,128)(2,1)S(1)}, f32[32,512]{1,0:T(8,128)S(1)}, f32[32,512]{1,0:T(8,128)S(1)}) custom-call(s32[64]{0:T(128)S(1)} %copy-done.7, s32[64]{0:T(128)S(1)} %copy-done.8, bf16[512,128]{1,0:T(8,128)(2,1)S(1)} %bitcast.10, bf16[512,128]{1,0:T(8,128)(2,1)S(1)} %bitcast.11, f32[7,7,128]{2,1,0:T(8,128)S(1)} %copy-done.3, ...), custom_call_target="tpu_custom_call" | custom-call | tf_op jit(solution)/shard_map/block/pallas_call | solution.py:378
  74.0 0.7 copy.20
  74.6 0.6 copy.21
  75.3 0.6 copy.22
Async XLA Ops:
  0.6 1.1 %copy-start = (bf16[2,16,16,128]{3,2,1,0:T(8,128)(2,1)S(1)}, bf16[2,16,16,128]{3,2,1,0:T(8,128)(2,1)}, u32[]{:S(2)}) copy-start(bf16[2,16,16,128]{3,2,1,0:T(8,128)(2,1)} %param.13) | copy-start | bytes 393220
  0.6 1.1 %copy-start.2 = (bf16[32,512]{1,0:T(8,128)(2,1)S(1)}, bf16[32,512]{1,0:T(8,128)(2,1)}, u32[]{:S(2)}) copy-start(bf16[32,512]{1,0:T(8,128)(2,1)} %w_in.1) | copy-start | bytes 98308
  0.7 1.1 %copy-start.4 = (f32[1024]{0:T(1024)S(1)}, f32[1024]{0:T(1024)}, u32[]{:S(2)}) copy-start(f32[1024]{0:T(1024)} %param.18) | copy-start | bytes 12292
  0.7 1.1 %copy-start.5 = (f32[1024]{0:T(1024)S(1)}, f32[1024]{0:T(1024)}, u32[]{:S(2)}) copy-start(f32[1024]{0:T(1024)} %param.19) | copy-start | bytes 12292
  0.7 1.1 %copy-start.6 = (f32[512]{0:T(512)S(1)}, f32[512]{0:T(512)}, u32[]{:S(2)}) copy-start(f32[512]{0:T(512)} %param.21) | copy-start | bytes 6148
  0.7 1.1 %copy-start.7 = (s32[64]{0:T(128)S(1)}, s32[64]{0:T(128)}, u32[]{:S(2)}) copy-start(s32[64]{0:T(128)} %slot_tile.1) | copy-start | bytes 772
  0.7 1.1 %copy-start.8 = (s32[64]{0:T(128)S(1)}, s32[64]{0:T(128)}, u32[]{:S(2)}) copy-start(s32[64]{0:T(128)} %land.1) | copy-start | bytes 772
  0.7 1.1 %copy-start.9 = (f32[128]{0:T(128)S(1)}, f32[128]{0:T(128)}, u32[]{:S(2)}) copy-start(f32[128]{0:T(128)} %param.17) | copy-start | bytes 1540
  0.7 1.1 %copy-start.10 = (f32[128]{0:T(128)S(1)}, f32[128]{0:T(128)}, u32[]{:S(2)}) copy-start(f32[128]{0:T(128)} %param.23) | copy-start | bytes 1540
  0.7 1.1 %copy-start.11 = (f32[128]{0:T(128)S(1)}, f32[128]{0:T(128)}, u32[]{:S(2)}) copy-start(f32[128]{0:T(128)} %param.24) | copy-start | bytes 1540
  1.8 0.9 %copy-start.1 = (bf16[2,16,16,128]{3,2,1,0:T(8,128)(2,1)S(1)}, bf16[2,16,16,128]{3,2,1,0:T(8,128)(2,1)}, u32[]{:S(2)}) copy-start(bf16[2,16,16,128]{3,2,1,0:T(8,128)(2,1)} %param.25) | copy-start | bytes 393220
  2.7 0.7 copy-start.3

commit v2 on v1

v2 whole, which is shorter than its diff:
```python
import jax
import jax.numpy as jnp
from jax import lax
from jax.experimental import pallas as pl
from jax.experimental.pallas import tpu as pltpu
from jax.sharding import PartitionSpec as P

MESH = pl.DeviceIdType.MESH
F32, BF16 = jnp.float32, jnp.bfloat16
FAR = (1, 3, 2)
COPIES = 120


def wrap4(value):
    return lax.rem(value + 4, 4)


class Place:
    def __init__(self):
        self.space, self.chan = lax.axis_index("space"), lax.axis_index("chan")
        self.x, self.zh, self.core = self.space // 8, (self.space // 2) % 4, self.space % 2
        self.zl, self.y = self.chan // 4, self.chan % 4

    def slot(self, dx=0, dz=0, other=False):
        core = 1 - self.core if other else self.core
        return wrap4(self.x + dx) * 8 + wrap4(self.zh + dz) * 2 + core

    def part(self, dy=0, other=False):
        return (1 - self.zl if other else self.zl) * 4 + wrap4(self.y + dy)

    def ahead_x(self, d):
        return self.slot(dx=d), self.chan

    def ahead_z(self, d):
        return self.slot(dz=d), self.chan

    def ahead_y(self, d):
        return self.space, self.part(dy=d)

    def other_core(self):
        return self.slot(other=True), self.chan

    def other_zl(self):
        return self.space, self.part(other=True)

    def across(self, d):
        return self.slot(dx=d, other=True), self.chan

    def peers(self):
        ahead = (self.ahead_x, self.ahead_z, self.ahead_y, self.across)
        return [f(d) for f in ahead for d in FAR] + [self.other_core(), self.other_zl()]


class Links:
    def __init__(self, send_sems, recv_sems):
        self.send_sems, self.recv_sems, self.sent = send_sems, recv_sems, []

    def describe(self, number, source, target, device):
        return pltpu.make_async_remote_copy(
            src_ref=source,
            dst_ref=target,
            send_sem=self.send_sems.at[number],
            recv_sem=self.recv_sems.at[number],
            device_id=device,
            device_id_type=MESH,
        )

    def start(self, source, target, device):
        number = len(self.sent)
        assert number < COPIES
        copy = self.describe(number, source, target, device)
        copy.start()
        self.sent.append(copy)
        return number, device

    def landed(self, ticket, where):
        self.describe(ticket[0], where, where, ticket[1]).wait_recv()

    def finish(self):
        for copy in self.sent:
            copy.wait_send()


class SpaceGather:
    def __init__(self, links, place, block):
        self.links, self.place, self.block = links, place, block
        self.over_z, self.over_x, self.over_core = {}, {}, {}

    def send(self, block, device):
        return self.links.start(block, block, device)

    def own_z(self):
        place = self.place
        mine = self.block(place.slot())
        for d in FAR:
            self.over_z[d] = self.send(mine, (place.slot(dz=d), place.chan))

    def spread(self, d):
        place = self.place
        block = self.block(place.slot(dz=-d))
        if d:
            self.links.landed(self.over_z[d], block)
        for e in FAR:
            self.over_x[d, e] = self.send(block, (place.slot(dx=e), place.chan))
        self.over_core[d, 0] = self.send(block, (place.slot(other=True), place.chan))

    def cross(self, d, e):
        place = self.place
        block = self.block(place.slot(dx=-e, dz=-d))
        self.links.landed(self.over_x[d, e], block)
        self.over_core[d, e] = self.send(block, (place.slot(other=True), place.chan))

    def wait(self):
        place = self.place
        for (d, e), ticket in self.over_core.items():
            self.links.landed(ticket, self.block(place.slot(dx=-e, dz=-d, other=True)))


class ChanGather:
    def __init__(self, links, place, block):
        self.links, self.place, self.block = links, place, block
        self.over_y = {}

    def own_zl(self):
        mine = self.block(self.place.part())
        self.over_zl = self.links.start(mine, mine, self.place.other_zl())

    def own_y(self):
        self.spread(self.block(self.place.part()), False)

    def spread(self, block, other):
        place = self.place
        for d in FAR:
            self.over_y[d, other] = self.links.start(block, block, (place.space, place.part(dy=d)))

    def cross(self):
        block = self.block(self.place.part(other=True))
        self.links.landed(self.over_zl, block)
        self.spread(block, True)

    def wait(self):
        for (d, other), ticket in self.over_y.items():
            self.links.landed(ticket, self.block(self.place.part(dy=-d, other=other)))


class ChanGatherY(ChanGather):
    def cross(self):
        self.over_z = {}
        for d in FAR:
            block = self.block(self.place.part(dy=-d))
            self.links.landed(self.over_y[d, False], block)
            self.over_z[d] = self.links.start(block, block, self.place.other_zl())

    def wait(self):
        self.links.landed(self.over_zl, self.block(self.place.part(other=True)))
        for d in FAR:
            self.links.landed(self.over_z[d], self.block(self.place.part(dy=-d, other=True)))


class RingSum:
    def __init__(self, links, ahead, part, held):
        self.links, self.ahead, self.part, self.held = links, ahead, part, held
        self.tickets = {}

    def send(self, name, value, source, target, k):
        self.held[source] = value.astype(BF16)
        self.tickets[name] = self.links.start(
            self.held.at[source], self.held.at[target], self.ahead(k)
        )

    def take(self, name, where):
        self.links.landed(self.tickets[name], self.held.at[where])
        return self.held[where].astype(F32)

    def far(self):
        self.send("far0", self.part(2, 0), 0, 2, 1)
        self.send("far1", self.part(2, 1), 1, 3, 3)

    def near(self):
        self.send((0, 1), self.part(1, 1), 5, 9, 1)
        self.send((1, 0), self.part(3, 0), 6, 10, 3)

    def relay(self):
        self.send((0, 0), self.part(1, 0) + self.take("far0", 2), 4, 8, 1)
        self.send((1, 1), self.part(3, 1) + self.take("far1", 3), 7, 11, 3)

    def total(self, h):
        return self.part(0, h) + self.take((0, h), 8 + h) + self.take((1, h), 10 + h)


class DirectSum:
    def __init__(self, links, ahead, part, held):
        self.links, self.ahead, self.part, self.held = links, ahead, part, held
        self.tickets = {}

    def start(self):
        for k in FAR:
            self.held[k - 1] = self.part(k).astype(BF16)
            self.tickets[k] = self.links.start(
                self.held.at[k - 1], self.held.at[k + 2], self.ahead(k)
            )

    def total(self):
        total = self.part(0)
        for k in FAR:
            self.links.landed(self.tickets[k], self.held.at[k + 2])
            total = total + self.held[k + 2].astype(F32)
        return total


def kernel(
    slot_tile, land, feat_in, cot_in, dw_in, dw_bias_in, gain_in, shift_in, w_in, b_in_in, w_out_in,
    b_out_in, scale_in,
    out, gin, gout,
    feat, cot, dw, dw_bias, gain, shift, b_in, b_out, scale,
    xpad, cacc, hbuf, hsel, hsend, hrecv, hacc, wbuf, sbuf, dbuf0, dbuf1, nbuf, pre, qbuf, hid, back,
    gacc, gsend, gcore, gx, gown, gz, mx, mown, mzs, mzr,
    load_sems, send_sems, recv_sems,
):
    place, links = Place(), Links(send_sems, recv_sems)
    core, zl = place.core, place.zl
    first = place.space * 2
    barrier = pltpu.get_barrier_semaphore()
    for peer in place.peers():
        pl.semaphore_signal(barrier, inc=1, device_id=peer, device_id_type=MESH)
    loads = {}
    for name, source, target in (
        ("feat", feat_in, feat),
        ("scale", scale_in, scale),
        ("cot", cot_in, cot),
        ("w_in", w_in, wbuf.at[place.space, 0]),
        ("w_out", w_out_in, wbuf.at[place.space, 1]),
        ("dw", dw_in, dw),
        ("dw_bias", dw_bias_in, dw_bias),
        ("gain", gain_in, gain),
        ("shift", shift_in, shift),
        ("b_in", b_in_in, b_in),
        ("b_out", b_out_in, b_out),
    ):
        loads[name] = pltpu.make_async_copy(source, target, load_sems.at[len(loads)])
        loads[name].start()

    xpad[...] = jnp.zeros((2, 22, 32, 128), F32)
    hacc[...] = jnp.zeros((2, 2, 3, 32, 128), F32)
    tiles = [slot_tile[first + t] for t in range(2)]
    lands = [land[tile].astype(F32) for tile in tiles]
    loads["feat"].wait()
    for t in range(2):
        masked = feat[t * 256 : (t + 1) * 256, :].astype(F32) * lands[t]
        xpad[t, 3:19, 8:24, :] = masked.reshape(16, 16, 128)
        for side, begin in ((0, 0), (1, 13)):
            for q in range(3):
                column = xpad[t, 3:19, 8 + begin + q, :]
                hbuf[0, t * 2 + side, q] = column.astype(BF16)
    pl.semaphore_wait(barrier, len(place.peers()))

    dests = [(d, other) for other in (False, True) for d in range(4)]
    wanted = [
        [slot_tile[place.slot(dx=d, other=other) * 2 + t] for t in range(2)] for d, other in dests
    ]

    def pick(k):
        held = [slot_tile[place.slot(dz=-k) * 2 + i] for i in range(2)]
        strips = [hbuf[k, i].astype(F32) for i in range(4)]
        for n in range(8):
            for t in range(2):
                for side, step in ((0, -1), (1, 1)):
                    chosen = [(held[i] == wanted[n][t] + step).astype(F32) for i in range(2)]
                    found = strips[1 - side] * chosen[0] + strips[3 - side] * chosen[1]
                    if k:
                        found = found + hsel[n, t, side]
                    hsel[n, t, side] = found

    weights = SpaceGather(links, place, lambda s: wbuf.at[s])
    slopes = ChanGather(links, place, lambda c: sbuf.at[c])
    dbufs = (dbuf0, dbuf1)
    convs = [
        kind(links, place, lambda c, held=held: held.at[c])
        for kind, held in zip((ChanGather, ChanGatherY), dbufs)
    ]

    halo_z = {d: links.start(hbuf.at[0], hbuf.at[d], place.ahead_z(d)) for d in FAR}
    loads["scale"].wait()
    loads["cot"].wait()
    for t in range(2):
        rows = slice(t * 256, (t + 1) * 256)
        sbuf[place.chan, rows] = (cot[rows, :].astype(F32) * lands[t] * scale[...]).astype(BF16)
    slopes.own_y()
    slopes.own_zl()
    for name in ("w_in", "w_out"):
        loads[name].wait()
    weights.spread(0)
    pick(0)

    for name in ("dw", "dw_bias"):
        loads[name].wait()

    def inner(n, carry):
        t, i = n // 2, n % 2
        total = jnp.zeros((8, 16, 128), F32) + dw_bias[...][None]
        for e in range(7):
            rows = xpad[t, pl.ds(i * 8, 14), 5 + e : 21 + e, :]
            for a in range(7):
                total = total + dw[a, e : e + 1, :][None] * rows[a : a + 8]
        cacc[t, pl.ds(i * 8, 8)] = total
        return carry

    lax.fori_loop(0, 4, inner, 0)
    for d in FAR:
        links.landed(halo_z[d], hbuf.at[d])
        pick(d)
    halo_x = {}
    for n in (5, 7, 1, 3, 6, 2, 4):
        d, other = dests[n]
        hsend[n] = hsel[n].astype(BF16)
        device = place.across(d) if other else place.ahead_x(d)
        halo_x[n] = links.start(hsend.at[n], hrecv.at[n], device)
    slopes.cross()
    weights.own_z()
    for t in range(2):
        for side in range(2):
            hacc[t, side, :, 8:24] = hsel[0, t, side]
    for n, ticket in halo_x.items():
        links.landed(ticket, hrecv.at[n])
        for t in range(2):
            for side in range(2):
                hacc[t, side, :, 8:24] += hrecv[n, t, side].astype(F32)

    for t in range(2):
        for side in range(2):
            for q in range(3):
                total = jnp.zeros((16, 128), F32)
                for j in range(q, 3) if side == 0 else range(q + 1):
                    e = j - q if side == 0 else 6 + j - q
                    for a in range(7):
                        total = total + dw[a, e : e + 1, :] * hacc[t, side, j, 5 + a : 21 + a]
                cacc[t, :, 13 * side + q, :] += total
        dbufs[t][place.chan] = cacc[t].reshape(256, 128).astype(BF16)
        if t:
            convs[t].own_y()
            convs[t].own_zl()
        else:
            convs[t].own_zl()
            convs[t].own_y()

    for d in (1, 3):
        weights.spread(d)
    convs[0].cross()
    weights.spread(2)
    convs[1].cross()
    for d in (0,) + FAR:
        for e in FAR:
            weights.cross(d, e)
    slopes.wait()
    weights.wait()
    for name in ("gain", "shift", "b_in", "b_out"):
        loads[name].wait()

    for t in range(2):
        rows = slice(t * 256, (t + 1) * 256)
        slope_rows = jnp.concatenate([sbuf[c, rows] for c in range(8)], axis=1)
        qbuf[rows] = jnp.dot(
            slope_rows, wbuf[:, 1].reshape(1024, 512), preferred_element_type=F32
        )

    for t in range(2):
        convs[t].wait()

        def norm(i, carry):
            at = pl.ds(pl.multiple_of(i * 64, 64), 64)
            x = dbufs[t][:, at, :].astype(F32)
            mean = jnp.sum(jnp.sum(x, axis=0), axis=1, keepdims=True) * (1.0 / 1024)
            x = x - mean[None]
            spread = jnp.sum(jnp.sum(x * x, axis=0), axis=1, keepdims=True) * (1.0 / 1024)
            x = x * lax.rsqrt(spread + 1e-06)[None]
            to = pl.ds(pl.multiple_of(t * 256 + i * 64, 64), 64)
            for c in range(8):
                y = x[c] * gain[c : c + 1] + shift[c : c + 1]
                nbuf[to, c * 128 : (c + 1) * 128] = y.astype(BF16)
            return carry

        lax.fori_loop(0, 4, norm, 0)
        rows = slice(t * 256, (t + 1) * 256)
        pre[...] = (
            jnp.dot(nbuf[rows], wbuf[:, 0].reshape(1024, 512), preferred_element_type=F32)
            + b_in[...]
        )

        def act(i, carry):
            at = pl.ds(pl.multiple_of(i * 32, 32), 32)
            to = pl.ds(pl.multiple_of(t * 256 + i * 32, 32), 32)
            p = pre[at]
            below = 0.5 * (1.0 + lax.erf(p * 0.7071067811865476))
            hid[to] = (p * below).astype(BF16)
            rise = below + p * jnp.exp(-0.5 * p * p) * 0.3989422804014327
            back[to] = (qbuf[to] * rise).astype(BF16)
            return carry

        lax.fori_loop(0, 8, act, 0)

    over_core = {}
    for g in (1, 0):
        for i in range(4):
            if g:
                left = jnp.concatenate((sbuf[2 * i], sbuf[2 * i + 1]), axis=1)
            else:
                left = nbuf[:, i * 256 : (i + 1) * 256]
            summed = lax.dot_general(
                left, (hid if g else back)[...], (((0,), (0,)), ((), ())),
                preferred_element_type=F32,
            )
            gacc[g, 4 * i : 4 * i + 4] = summed.reshape(4, 2, 32, 512)
            gsend[g, 4 * i : 4 * i + 4] = gacc[g, 4 * i : 4 * i + 4, 1 - core].astype(BF16)
        over_core[g] = links.start(gsend.at[g], gcore.at[g], place.other_core())

    def grad_part(g):
        def part(k, h):
            at = pl.ds(wrap4(place.x + k) * 4 + 2 * h, 2)
            return gacc[g, at, core] + gcore[g, at].astype(F32)

        return part

    over_x = [RingSum(links, place.ahead_x, grad_part(g), gx.at[g]) for g in range(2)]
    over_z = [
        DirectSum(
            links, place.ahead_z, lambda k, g=g: gown[g, wrap4(place.zh + k)], gz.at[g]
        )
        for g in range(2)
    ]
    for g in (1, 0):
        links.landed(over_core[g], gcore.at[g])
        over_x[g].far()
        if g:
            over_x[g].near()

    for k in (2, 1, 3, 0):
        to = wrap4(place.y + k)
        columns = jnp.concatenate(
            [wbuf[pl.ds(i * 16 + to * 4, 4), 1].reshape(128, 512) for i in range(2)], axis=0
        )
        partial = lax.dot_general(
            hid[...], columns, (((1,), (1,)), ((), ())), preferred_element_type=F32
        )
        for t in range(2):
            for i in range(2):
                mown[k, t, i] = partial[t * 256 : (t + 1) * 256, i * 128 : (i + 1) * 128]
    over_y = RingSum(links, place.ahead_y, lambda k, h: mown[k, h], mx)
    over_y.far()
    over_y.near()
    over_x[1].relay()
    over_x[0].near()
    over_x[0].relay()
    over_y.relay()
    for g in (1, 0):
        for h in range(2):
            gown[g, 2 * h : 2 * h + 2] = over_x[g].total(h)
        over_z[g].start()
    for t in range(2):
        mown[0, t] = over_y.total(t)
        mzs[t] = mown[0, t, 1 - zl].astype(BF16)
    mixed_z = links.start(mzs, mzr, place.other_zl())
    links.landed(mixed_z, mzr)
    for t in range(2):
        rows = slice(t * 256, (t + 1) * 256)
        mixed = mown[0, t, zl] + mzr[t].astype(F32)
        value = feat[rows, :].astype(F32) + scale[...] * (mixed + b_out[...])
        out[rows, :] = (lands[t] * value).astype(BF16)
    for g, result in ((1, gout), (0, gin)):
        result[...] = over_z[g].total()
    links.finish()


def body(
    features, slot_tile, land, dw_kernel, dw_bias, ln_gain, ln_bias, w_in, b_in, w_out, b_out,
    layer_scale, cotangent,
):
    vmem = pl.BlockSpec(memory_space=pltpu.VMEM)
    smem = pl.BlockSpec(memory_space=pltpu.SMEM)
    scratch = [
        ((512, 128), BF16),
        ((512, 128), BF16),
        ((7, 7, 128), F32),
        ((1, 128), F32),
        ((8, 128), F32),
        ((8, 128), F32),
        ((1, 512), F32),
        ((1, 128), F32),
        ((1, 128), F32),
        ((2, 22, 32, 128), F32),
        ((2, 16, 16, 128), F32),
        ((4, 4, 3, 16, 128), BF16),
        ((8, 2, 2, 3, 16, 128), F32),
        ((8, 2, 2, 3, 16, 128), BF16),
        ((8, 2, 2, 3, 16, 128), BF16),
        ((2, 2, 3, 32, 128), F32),
        ((32, 2, 32, 512), BF16),
        ((8, 512, 128), BF16),
        ((8, 256, 128), BF16),
        ((8, 256, 128), BF16),
        ((512, 1024), BF16),
        ((256, 512), F32),
        ((512, 512), F32),
        ((512, 512), BF16),
        ((512, 512), BF16),
        ((2, 16, 2, 32, 512), F32),
        ((2, 16, 32, 512), BF16),
        ((2, 16, 32, 512), BF16),
        ((2, 12, 2, 32, 512), BF16),
        ((2, 4, 32, 512), F32),
        ((2, 6, 32, 512), BF16),
        ((12, 2, 256, 128), BF16),
        ((4, 2, 2, 256, 128), F32),
        ((2, 256, 128), BF16),
        ((2, 256, 128), BF16),
    ]
    output, grad_in, grad_out = pl.pallas_call(
        kernel,
        out_shape=(
            jax.ShapeDtypeStruct((512, 128), BF16),
            jax.ShapeDtypeStruct((32, 512), F32),
            jax.ShapeDtypeStruct((32, 512), F32),
        ),
        in_specs=[smem, smem] + [pl.BlockSpec(memory_space=pltpu.HBM)] * 11,
        out_specs=(vmem, vmem, vmem),
        scratch_shapes=[pltpu.VMEM(shape, dtype) for shape, dtype in scratch]
        + [pltpu.SemaphoreType.DMA((11,)), pltpu.SemaphoreType.DMA((COPIES,)), pltpu.SemaphoreType.DMA((COPIES,))],
        compiler_params=pltpu.CompilerParams(
            collective_id=0, has_side_effects=True, vmem_limit_bytes=60 * 2**20
        ),
        name="block",
    )(
        slot_tile,
        land,
        features.reshape(512, 128),
        cotangent.reshape(512, 128),
        dw_kernel,
        dw_bias.reshape(1, 128),
        ln_gain.reshape(8, 128),
        ln_bias.reshape(8, 128),
        w_in,
        b_in.reshape(1, 512),
        w_out.T,
        b_out.reshape(1, 128),
        layer_scale.reshape(1, 128),
    )
    return output.reshape(features.shape), grad_in, grad_out.T


def solution(mesh):
    return jax.shard_map(
        body,
        mesh=mesh,
        in_specs=(
            P("space", None, None, "chan"),
            P(),
            P(),
            P(None, None, "chan"),
            P("chan"),
            P(),
            P(),
            P("space", "chan"),
            P("chan"),
            P("chan", "space"),
            P("chan"),
            P("chan"),
            P("space", None, None, "chan"),
        ),
        out_specs=(P("space", None, None, "chan"), P("space", "chan"), P("chan", "space")),
        check_vma=False,
    )
```

time: 77 us -> 68.2 us (0.89); the launches traced: 75.9 us -> 68 us
  Pallas kernels: 70.5 us -> 64.3 us
  local copies, waits for them, and re-layouts: 4.59 us -> 3.1 us
    pallas_call x1, Pallas kernels: 70.5 us -> 64.3 us  [body(): pl.pallas_call(kernel, out_shape=(jax.ShapeDtypeStruct((512, 128), BF16),...]
    unnamed x28 -> x7, local copies, waits for them, and re-layouts: 4.59 us -> 3.1 us
where the time goes in v2:
time: 68.2 us; the launch traced here: 68 us
  Pallas kernels  64.3 us (94%)
  local copies, waits for them, and re-layouts  3.1 us (5%)
    pallas_call x1, Pallas kernels, body(): pl.pallas_call(kernel, out_shape=(jax.ShapeDtypeStruct((512, 128), BF16),...  64.3 us
    unnamed x7, local copies, waits for them, and re-layouts  3.1 us

profile of v2, /device:TPU:1, one launch (start us, length us, event | category | flops | bytes accessed | tf_op | source)
XLA Modules:
  0.0 68.0 jit_solution(17593791251446686048)
XLA Ops:
  0.6 64.3 %block.1 = (bf16[512,128]{1,0:T(8,128)(2,1)}, f32[32,512]{1,0:T(8,128)}, f32[32,512]{1,0:T(8,128)}) custom-call(s32[64]{0:T(128)} %slot_tile.1, s32[64]{0:T(128)} %land.1, bf16[512,128]{1,0:T(8,128)(2,1)} %bitcast.11, bf16[512,128]{1,0:T(8,128)(2,1)} %bitcast.12, f32[7,7,128]{2,1,0:T(8,128)} %dw_in.1, f32[1,128]{1,0:T(1,128)} %bitcast.19, ...), custom_call_target="tpu_custom_call" | custom-call | tf_op jit(solution)/shard_map/block/pallas_call | solution.py:516
  64.9 0.0 copy-start.1
  64.9 1.6 %copy.19 = bf16[2,16,16,128]{3,2,1,0:T(8,128)(2,1)} copy(bf16[2,16,16,128]{3,2,1,0:T(8,128)(2,1)} %bitcast.13) | data formatting | bytes 262144
  66.5 0.0 copy-done.1
  66.5 0.0 copy-start
  66.5 0.6 copy.20
  67.2 0.2 copy-done
  67.4 0.6 copy.21
Async XLA Ops:
  64.9 1.6 %copy-start.1 = (f32[32,512]{1,0:T(8,128)S(1)}, f32[32,512]{1,0:T(8,128)}, u32[]{:S(2)}) copy-start(f32[32,512]{1,0:T(8,128)} %get-tuple-element.13) | copy-start | bytes 196612
  66.5 0.9 %copy-start = (f32[32,512]{1,0:T(8,128)S(1)}, f32[32,512]{1,0:T(8,128)}, u32[]{:S(2)}) copy-start(f32[32,512]{1,0:T(8,128)} %get-tuple-element.8) | copy-start | bytes 196612

commit v3 on v2

--- a/solution.py
+++ b/solution.py
@@ -450,11 +450,12 @@
     over_x[1].relay()
     over_x[0].near()
     over_x[0].relay()
-    over_y.relay()
     for g in (1, 0):
         for h in range(2):
             gown[g, 2 * h : 2 * h + 2] = over_x[g].total(h)
         over_z[g].start()
+        if g:
+            over_y.relay()
     for t in range(2):
         mown[0, t] = over_y.total(t)
         mzs[t] = mown[0, t, 1 - zl].astype(BF16)

time: 68.2 us -> 67.8 us (level)
  no operation moved by 1% of the time
where the time goes in v3:
time: 67.8 us; the launch traced here: 67.6 us
  Pallas kernels  63.8 us (94%)
  local copies, waits for them, and re-layouts  3.1 us (5%)
    pallas_call x1, Pallas kernels, body(): pl.pallas_call(kernel, out_shape=(jax.ShapeDtypeStruct((512, 128), BF16),...  63.8 us
    unnamed x7, local copies, waits for them, and re-layouts  3.1 us

profile of v3, /device:TPU:1, one launch (start us, length us, event | category | flops | bytes accessed | tf_op | source)
XLA Modules:
  0.0 67.6 jit_solution(287148627330459941)
XLA Ops:
  0.6 63.8 %block.1 = (bf16[512,128]{1,0:T(8,128)(2,1)}, f32[32,512]{1,0:T(8,128)}, f32[32,512]{1,0:T(8,128)}) custom-call(s32[64]{0:T(128)} %slot_tile.1, s32[64]{0:T(128)} %land.1, bf16[512,128]{1,0:T(8,128)(2,1)} %bitcast.11, bf16[512,128]{1,0:T(8,128)(2,1)} %bitcast.12, f32[7,7,128]{2,1,0:T(8,128)} %dw_in.1, f32[1,128]{1,0:T(1,128)} %bitcast.19, ...), custom_call_target="tpu_custom_call" | custom-call | tf_op jit(solution)/shard_map/block/pallas_call | solution.py:517
  64.5 0.0 copy-start.1
  64.5 1.6 %copy.19 = bf16[2,16,16,128]{3,2,1,0:T(8,128)(2,1)} copy(bf16[2,16,16,128]{3,2,1,0:T(8,128)(2,1)} %bitcast.13) | data formatting | bytes 262144
  66.1 0.0 copy-done.1
  66.1 0.0 copy-start
  66.1 0.6 copy.20
  66.7 0.2 copy-done
  67.0 0.6 copy.21
Async XLA Ops:
  64.5 1.6 %copy-start.1 = (f32[32,512]{1,0:T(8,128)S(1)}, f32[32,512]{1,0:T(8,128)}, u32[]{:S(2)}) copy-start(f32[32,512]{1,0:T(8,128)} %get-tuple-element.13) | copy-start | bytes 196612
  66.1 0.9 %copy-start = (f32[32,512]{1,0:T(8,128)S(1)}, f32[32,512]{1,0:T(8,128)}, u32[]{:S(2)}) copy-start(f32[32,512]{1,0:T(8,128)} %get-tuple-element.8) | copy-start | bytes 196612

commit v4 on v3

--- a/solution.py
+++ b/solution.py
@@ -411,7 +411,9 @@
             )
             gacc[g, 4 * i : 4 * i + 4] = summed.reshape(4, 2, 32, 512)
             gsend[g, 4 * i : 4 * i + 4] = gacc[g, 4 * i : 4 * i + 4, 1 - core].astype(BF16)
-        over_core[g] = links.start(gsend.at[g], gcore.at[g], place.other_core())
+        for k in (2, 1, 3, 0):
+            at = pl.ds(wrap4(place.x + k) * 4, 4)
+            over_core[g, k] = links.start(gsend.at[g, at], gcore.at[g, at], place.other_core())
 
     def grad_part(g):
         def part(k, h):
@@ -428,8 +430,10 @@
         for g in range(2)
     ]
     for g in (1, 0):
-        links.landed(over_core[g], gcore.at[g])
-        over_x[g].far()
+        for k in (2, 1, 3, 0):
+            links.landed(over_core[g, k], gcore.at[g, pl.ds(wrap4(place.x + k) * 4, 4)])
+            if k == 2:
+                over_x[g].far()
         if g:
             over_x[g].near()
 

time: 67.8 us -> 67.1 us (0.990)
  Pallas kernels: 63.8 us -> 63.1 us
    pallas_call x1, Pallas kernels: 63.8 us -> 63.1 us  [body(): pl.pallas_call(kernel, out_shape=(jax.ShapeDtypeStruct((512, 128), BF16),...]
where the time goes in v4:
time: 67.1 us; the launch traced here: 66.9 us
  Pallas kernels  63.1 us (94%)
  local copies, waits for them, and re-layouts  3.1 us (5%)
    pallas_call x1, Pallas kernels, body(): pl.pallas_call(kernel, out_shape=(jax.ShapeDtypeStruct((512, 128), BF16),...  63.1 us
    unnamed x7, local copies, waits for them, and re-layouts  3.1 us

profile of v4, /device:TPU:1, one launch (start us, length us, event | category | flops | bytes accessed | tf_op | source)
XLA Modules:
  0.0 66.9 jit_solution(9028185583763298671)
XLA Ops:
  0.6 63.1 %block.1 = (bf16[512,128]{1,0:T(8,128)(2,1)}, f32[32,512]{1,0:T(8,128)}, f32[32,512]{1,0:T(8,128)}) custom-call(s32[64]{0:T(128)} %slot_tile.1, s32[64]{0:T(128)} %land.1, bf16[512,128]{1,0:T(8,128)(2,1)} %bitcast.11, bf16[512,128]{1,0:T(8,128)(2,1)} %bitcast.12, f32[7,7,128]{2,1,0:T(8,128)} %dw_in.1, f32[1,128]{1,0:T(1,128)} %bitcast.19, ...), custom_call_target="tpu_custom_call" | custom-call | tf_op jit(solution)/shard_map/block/pallas_call | solution.py:521
  63.8 0.0 copy-start.1
  63.8 1.6 %copy.19 = bf16[2,16,16,128]{3,2,1,0:T(8,128)(2,1)} copy(bf16[2,16,16,128]{3,2,1,0:T(8,128)(2,1)} %bitcast.13) | data formatting | bytes 262144
  65.4 0.0 copy-done.1
  65.4 0.0 copy-start
  65.4 0.6 copy.20
  66.0 0.2 copy-done
  66.3 0.6 copy.21
Async XLA Ops:
  63.8 1.6 %copy-start.1 = (f32[32,512]{1,0:T(8,128)S(1)}, f32[32,512]{1,0:T(8,128)}, u32[]{:S(2)}) copy-start(f32[32,512]{1,0:T(8,128)} %get-tuple-element.13) | copy-start | bytes 196612
  65.4 0.9 %copy-start = (f32[32,512]{1,0:T(8,128)S(1)}, f32[32,512]{1,0:T(8,128)}, u32[]{:S(2)}) copy-start(f32[32,512]{1,0:T(8,128)} %get-tuple-element.8) | copy-start | bytes 196612
